TPU v7x, 512 devices: a whole 4x4x16 slice. The times are simulated.
512 devices in a mesh: gx: 64 (over x, z), gy: 8 (over y, core).
Axes of the slice: x: 4, y: 4, z: 16, core: 2. Of those that a mesh axis runs over, the one named last changes fastest.
Arguments:
- snapshot: bfloat16 [3, 512, 128, 1024], P(None, 'gx', 'gy'), may hold values from -6 to 6
- basis: bfloat16 [3, 64, 16, 128, 512], P(None, 'gx', 'gy'), may hold values from -3000 to 3000
- taps: bfloat16 [3, 17], replicated, may hold values from 0.099609375 to 1
Outputs:
- new_modes: bfloat16 [3, 64, 16, 128, 512], P(None, 'gx', 'gy')
- new_mode: float32 [3, 64, 16, 128], P(None, 'gx', 'gy')
- factor: float32 [513, 513], replicated
All inputs are finite; a program needn't handle non-finite values.
Results may differ from a plain program's by a relative error of at most 0.0012.
The roundings to bfloat16 on the way count: a program that leaves them out, or rounds other values in their place, can miss the bound.
Values sent between devices are 32-bit elements; how exact they have to be, the bound alone decides.
A program may use at most 64 MiB of HBM per device.

v0:
```python
import jax
import jax.numpy as jnp
from jax import lax
from jax.sharding import PartitionSpec as P

STRIDE = 8


def padded(block, sides, width, periodic):
    for axis, dim in sides:
        count = lax.axis_size(axis)
        forward = [(i, i + 1) for i in range(count - 1)]
        if periodic:
            forward.append((count - 1, 0))
        backward = [(target, source) for source, target in forward]
        low = lax.ppermute(
            lax.slice_in_dim(block, block.shape[dim] - width, None, axis=dim), axis, forward
        )
        high = lax.ppermute(lax.slice_in_dim(block, 0, width, axis=dim), axis, backward)
        block = jnp.concatenate([low, block, high], axis=dim)
    return block


def band(taps_row, length, out_len, shift, wrap):
    rows = jnp.arange(length, dtype=jnp.int32)[:, None]
    cols = jnp.arange(out_len, dtype=jnp.int32)[None, :]
    lag = rows - STRIDE * cols + shift
    if wrap:
        lag = lag % length
    hits = lag[:, :, None] == jnp.arange(2 * STRIDE + 1, dtype=jnp.int32)[None, None, :]
    return jnp.sum(jnp.where(hits, taps_row[None, None, :], jnp.zeros((), taps_row.dtype)), axis=-1)


def local(snapshot, basis, taps):
    comps, cells_x, cells_y, cells_z = snapshot.shape
    modes = basis.shape[-1]
    flat_rows = basis.reshape(-1, modes)
    total = flat_rows.shape[0] * lax.axis_size("gx") * lax.axis_size("gy")
    matrix_z = band(taps[2], cells_z, cells_z // STRIDE, STRIDE, True)
    along_z = jnp.dot(snapshot.reshape(-1, cells_z), matrix_z, preferred_element_type=jnp.float32)
    along_z = along_z.reshape(comps, cells_x, cells_y, cells_z // STRIDE)
    padded_y = padded(along_z, (("gy", 2),), STRIDE, False)
    matrix_y = band(taps[1], cells_y + 2 * STRIDE, cells_y // STRIDE, 0, False).astype(jnp.float32)
    along_y = jnp.einsum("cxyz,yf->cxfz", padded_y, matrix_y, precision=lax.Precision.HIGHEST)
    padded_x = padded(along_y, (("gx", 1),), STRIDE, True)
    matrix_x = band(taps[0], cells_x + 2 * STRIDE, cells_x // STRIDE, 0, False).astype(jnp.float32)
    along_x = jnp.einsum("cxyz,xf->cfyz", padded_x, matrix_x, precision=lax.Precision.HIGHEST)
    filtered = along_x.astype(jnp.bfloat16).reshape(-1)
    stack = jnp.concatenate([flat_rows, filtered[:, None]], axis=1)
    gram = lax.psum(
        jnp.einsum("rk,rj->kj", stack, stack, preferred_element_type=jnp.float32), ("gx", "gy")
    )
    gram = gram / total
    lower = jnp.linalg.cholesky(gram)
    solved = lax.linalg.triangular_solve(
        lower, stack.astype(jnp.float32), left_side=False, lower=True, transpose_a=True
    )
    new_modes = solved[:, :modes].astype(jnp.bfloat16).reshape(basis.shape)
    new_mode = solved[:, modes].reshape(basis.shape[:-1])
    return (new_modes, new_mode, lower.T)


def solution(mesh):
    in_specs = (P(None, "gx", "gy", None), P(None, "gx", "gy", None, None), P())
    out_specs = (P(None, "gx", "gy", None, None), P(None, "gx", "gy", None), P())
    return jax.shard_map(local, mesh=mesh, in_specs=in_specs, out_specs=out_specs, check_vma=False)
```

profile of v0, /device:TPU:1, one launch (start us, length us, event | category | flops | bytes accessed | tf_op | source)
XLA Modules:
  0.0 709.4 jit_solution(6518800129823269705)
XLA Ops:
  7.2 0.8 slice_bitcast_fusion.14
  8.3 0.9 fusion.1
  9.8 4.6 collective-permute-start
  14.4 5.5 collective-permute-start.1
  21.1 3.1 collective-permute-start.2
  24.1 11.7 %collective-permute-start.3 = (f32[3,8,2,128]{3,2,1,0:T(2,128)S(1)}, f32[3,8,2,128]{3,2,1,0:T(2,128)S(1)}, u32[]{:S(2)}, u32[]{:S(2)}) collective-permute-start(f32[3,8,2,128]{3,2,1,0:T(2,128)S(1)} %convolution_bitcast_fusion.1), channel_id=1, source_target_pairs={{8,0},{16,8},{24,16},{32,24},{40,32},{48,40},{56,48},{64,56},{72,6... | collective-permute-start | bytes 73736 | tf_op jit(solution)/shard_map/ppermute | solution.py:19
  35.9 0.8 collective-permute-done.3
  37.3 1.9 fusion.25
  39.3 1.4 fusion.24
  40.7 462.9 %all-reduce.5.cloned.1.call-done = f32[513,513]{0,1:T(8,128)} async-done(((f32[513,513]{0,1:T(8,128)}), f32[513,513]{0,1:T(8,128)}) %all-reduce.5.cloned.1.call-update) | async-done | bytes 1052692 | tf_op jit(solution)/shard_map/psum | solution.py:50
  503.6 2.5 broadcast_multiply_fusion
  506.1 1.9 copy.56
  508.3 1.0 copy-done.4
  509.8 11.7 %cholesky.131 = f32[128,128]{1,0:T(8,128)S(1)} custom-call(f32[128,128]{1,0:T(8,128)S(1)} %cholesky.333), custom_call_target="Cholesky" | custom-call | tf_op jit(solution)/shard_map/jit(cholesky)/cholesky | solution.py:54
  521.6 9.8 %custom-call.35 = f32[1,128,128]{1,2,0:T(8,128)S(1)} custom-call(f32[1,128,128]{2,1,0:T(8,128)S(1)} %get-tuple-element.47), custom_call_target="InvertDiagBlocksLowerTriangular" | custom-call | tf_op jit(solution)/shard_map/jit(cholesky)/cholesky | solution.py:54
  531.5 1.4 constant_dynamic-update-slice_fusion.2
  532.9 1.4 convolution_subtract_fusion.3
  534.3 11.9 %cholesky.264 = f32[128,128]{1,0:T(8,128)S(1)} custom-call(f32[128,128]{1,0:T(8,128)S(1)} %cholesky.337), custom_call_target="Cholesky" | custom-call | tf_op jit(solution)/shard_map/jit(cholesky)/cholesky | solution.py:54
  546.2 9.8 %custom-call.36 = f32[1,128,128]{1,2,0:T(8,128)S(1)} custom-call(f32[1,128,128]{2,1,0:T(8,128)S(1)} %get-tuple-element.44), custom_call_target="InvertDiagBlocksLowerTriangular" | custom-call | tf_op jit(solution)/shard_map/jit(cholesky)/cholesky | solution.py:54
  556.4 1.3 convolution_subtract_fusion.4
  557.7 11.7 %cholesky.285 = f32[128,128]{1,0:T(8,128)S(1)} custom-call(f32[128,128]{1,0:T(8,128)S(1)} %cholesky.342), custom_call_target="Cholesky" | custom-call | tf_op jit(solution)/shard_map/jit(cholesky)/cholesky | solution.py:54
  569.5 9.8 %custom-call.37 = f32[1,128,128]{1,2,0:T(8,128)S(1)} custom-call(f32[1,128,128]{2,1,0:T(8,128)S(1)} %get-tuple-element.41), custom_call_target="InvertDiagBlocksLowerTriangular" | custom-call | tf_op jit(solution)/shard_map/jit(cholesky)/cholesky | solution.py:54
  579.5 1.3 convolution_subtract_fusion.5
  580.8 11.9 %cholesky.304 = f32[128,128]{1,0:T(8,128)S(1)} custom-call(f32[128,128]{1,0:T(8,128)S(1)} %cholesky.347), custom_call_target="Cholesky" | custom-call | tf_op jit(solution)/shard_map/jit(cholesky)/cholesky | solution.py:54
  592.8 9.8 %custom-call.38 = f32[1,128,128]{1,2,0:T(8,128)S(1)} custom-call(f32[1,128,128]{2,1,0:T(8,128)S(1)} %get-tuple-element.38), custom_call_target="InvertDiagBlocksLowerTriangular" | custom-call | tf_op jit(solution)/shard_map/jit(cholesky)/cholesky | solution.py:54
  609.5 1.3 fusion.20
  611.3 10.1 %while.1 = (s32[]{:T(128)}, f32[513,513]{1,0:T(8,128)S(1)}, s32[4,2]{0,1:T(2,128)S(1)}, f32[4,128,128]{2,1,0:T(8,128)}, s32[]{:T(128)}) while((s32[]{:T(128)}, f32[513,513]{1,0:T(8,128)S(1)}, s32[4,2]{0,1:T(2,128)S(1)}, f32[4,128,128]{2,1,0:T(8,128)}, s32[]{:T(128)}) %tuple.44), condition=%wide.while_cond, body=%wide.while_body.sunk | while | flops 2 | bytes 132705 | solution.py:55
  611.9 1.9 bitcast_dynamic-update-slice_fusion.2
  614.4 1.9 bitcast_dynamic-update-slice_fusion.2
  616.9 1.9 bitcast_dynamic-update-slice_fusion.2
  619.4 1.9 bitcast_dynamic-update-slice_fusion.2
  622.1 1.0 pad_maximum_fusion.3
  623.1 49.1 %custom-call.39 = f32[5,128,128]{1,2,0:T(8,128)S(1)} custom-call(f32[5,128,128]{2,1,0:T(8,128)S(1)} %pad_maximum_fusion.3), custom_call_target="InvertDiagBlocksLowerTriangular" | custom-call | tf_op jit(solution)/shard_map/triangular_solve | solution.py:55
  672.2 2.1 bitcast_convert_fusion
  674.8 2.0 convolution_subtract_fusion.1
  676.8 2.1 fusion.73
  678.9 1.2 copy.57
  680.1 2.3 convolution_subtract_fusion.2
  682.4 2.1 fusion.72
  684.5 1.9 copy.59
  686.4 3.1 convolution_subtract_fusion
  689.5 2.1 fusion.71
  691.6 1.9 copy.66
  693.5 2.0 fusion.17
  695.6 0.9 fusion.28
  697.1 1.1 copy.77
  698.2 2.9 copy.69
  701.2 1.0 pad_maximum_fusion.1
  (76 shorter events, 12.0 us)
Async XLA Ops:
  7.2 2.1 copy-start
  7.2 496.4 %all-reduce.5.cloned.1.call-start = ((), (), s32[]{:S(2)}) async-start(), calls=%async_computation | async-start | bytes 2662400 | tf_op jit(solution)/shard_map/psum | solution.py:50
  9.2 28.1 %copy-start.5 = (bf16[3,1,2,128,512]{4,3,2,1,0:T(8,128)(2,1)S(1)}, bf16[3,1,2,128,512]{4,3,2,1,0:T(8,128)(2,1)}, u32[]{:S(2)}) copy-start(bf16[3,1,2,128,512]{4,3,2,1,0:T(8,128)(2,1)} %param.4) | copy-start | bytes 2359300
  9.8 10.3 %collective-permute-start = (f32[3,8,8,128]{3,2,1,0:T(8,128)S(1)}, f32[3,8,8,128]{3,2,1,0:T(8,128)S(1)}, u32[]{:S(2)}, u32[]{:S(2)}) collective-permute-start(f32[3,8,8,128]{3,2,1,0:T(8,128)S(1)} %get-tuple-element.35), channel_id=1, source_target_pairs={{0,1},{1,2},{2,3},{3,4},{4,5},{5,6},{6,7},{8,9},{9,10},{10,11},{11... | collective-permute-start | bytes 294920 | tf_op jit(solution)/shard_map/ppermute | solution.py:16
  14.4 6.4 collective-permute-start.1
  21.1 14.9 %collective-permute-start.2 = (f32[3,8,2,128]{3,2,1,0:T(2,128)S(1)}, f32[3,8,2,128]{3,2,1,0:T(2,128)S(1)}, u32[]{:S(2)}, u32[]{:S(2)}) collective-permute-start(f32[3,8,2,128]{3,2,1,0:T(2,128)S(1)} %convolution_bitcast_fusion.1), channel_id=1, source_target_pairs={{0,8},{8,16},{16,24},{24,32},{32,40},{40,48},{48,56},{56,64},{64,7... | collective-permute-start | bytes 73736 | tf_op jit(solution)/shard_map/ppermute | solution.py:16
  24.1 12.6 %collective-permute-start.3 = (f32[3,8,2,128]{3,2,1,0:T(2,128)S(1)}, f32[3,8,2,128]{3,2,1,0:T(2,128)S(1)}, u32[]{:S(2)}, u32[]{:S(2)}) collective-permute-start(f32[3,8,2,128]{3,2,1,0:T(2,128)S(1)} %convolution_bitcast_fusion.1), channel_id=1, source_target_pairs={{8,0},{16,8},{24,16},{32,24},{40,32},{48,40},{56,48},{64,56},{72,6... | collective-permute-start | bytes 73736 | tf_op jit(solution)/shard_map/ppermute | solution.py:19
  506.1 1.9 copy-start.2
  508.2 1.1 copy-start.4
  621.4 53.5 %copy-start.3 = (f32[513,513]{1,0:T(8,128)}, f32[513,513]{1,0:T(8,128)S(1)}, u32[]{:S(2)}) copy-start(f32[513,513]{1,0:T(8,128)S(1)} %get-tuple-element.109) | copy-start | bytes 3158032
  672.2 2.6 copy-start.9
  674.8 5.2 copy-start.1
  698.2 3.0 copy-start.6
  698.2 2.9 copy-start.7
  698.2 2.9 copy-start.8
Sparse Core Ops, SparseCore 0:
  39.4 464.2 all-reduce.4
where the time goes:
time: 720 us; the launch traced here: 709 us
  waiting for transfers between devices  464 us (64%)
  other arithmetic  149 us (21%)
  matrix products  26.7 us (4%)
  local copies, waits for them, and re-layouts  25.8 us (4%)
  starting transfers between devices  24.9 us (3%)
  between operations  18.8 us (3%)
    psum x1, waiting for transfers between devices, local(): lax.psum(jnp.einsum('rk,rj->kj', stack, stack, preferred_element_type=jnp...  463 us
    another operation x16, other arithmetic, local(): lower = jnp.linalg.cholesky(gram)  89.2 us
    another operation x8, other arithmetic, local(): lax.linalg.triangular_solve(lower, stack.astype(jnp.float32), left_side=F...  52.8 us
    another operation x8, matrix products, local(): lax.linalg.triangular_solve(lower, stack.astype(jnp.float32), left_side=F...  17.8 us
    ppermute x2, starting transfers between devices, padded(): lax.ppermute(lax.slice_in_dim(block, 0, width, axis=dim), axis, backward)  17.2 us
  transfers between devices with their start and end apart: 5, of which 3 were waited for; matrix products, arithmetic and copies ran while one was open for 0% of the time, Pallas kernels for 0%

commit v1 on v0

--- a/solution.py
+++ b/solution.py
@@ -48,7 +48,8 @@
     filtered = along_x.astype(jnp.bfloat16).reshape(-1)
     stack = jnp.concatenate([flat_rows, filtered[:, None]], axis=1)
     gram = lax.psum(
-        jnp.einsum("rk,rj->kj", stack, stack, preferred_element_type=jnp.float32), ("gx", "gy")
+        lax.psum(jnp.einsum("rk,rj->kj", stack, stack, preferred_element_type=jnp.float32), "gx"),
+        "gy",
     )
     gram = gram / total
     lower = jnp.linalg.cholesky(gram)

time: 720 us -> 596 us (0.83)
  waiting for transfers between devices: 464 us -> 346 us
    psum x1, waiting for transfers between devices: 463 us -> 262 us  [local(): lax.psum(jnp.einsum('rk,rj->kj', stack, stack, preferred_element_type=jnp...]
    psum x0 -> x1, waiting for transfers between devices: none -> 82.2 us  [local(): lax.psum(lax.psum(jnp.einsum('rk,rj->kj', stack, stack, preferred_element...]
  transfers between devices with their start and end apart: 5 -> 6, of which waited for: 3 -> 4; matrix products, arithmetic and copies ran while one was open for 0% -> 0% of each run, Pallas kernels for 0% -> 0%
where the time goes in v1:
time: 596 us; the launch traced here: 592 us
  waiting for transfers between devices  346 us (58%)
  other arithmetic  149 us (25%)
  matrix products  26.7 us (4%)
  local copies, waits for them, and re-layouts  26.2 us (4%)
  starting transfers between devices  25.4 us (4%)
  between operations  18.6 us (3%)
    psum x1, waiting for transfers between devices, local(): lax.psum(jnp.einsum('rk,rj->kj', stack, stack, preferred_element_type=jnp...  262 us
    another operation x16, other arithmetic, local(): lower = jnp.linalg.cholesky(gram)  89.2 us
    psum x1, waiting for transfers between devices, local(): lax.psum(lax.psum(jnp.einsum('rk,rj->kj', stack, stack, preferred_element...  82.2 us
    another operation x8, other arithmetic, local(): lax.linalg.triangular_solve(lower, stack.astype(jnp.float32), left_side=F...  52.8 us
    another operation x8, matrix products, local(): lax.linalg.triangular_solve(lower, stack.astype(jnp.float32), left_side=F...  17.8 us
    ppermute x2, starting transfers between devices, padded(): lax.ppermute(lax.slice_in_dim(block, 0, width, axis=dim), axis, backward)  17.2 us
  transfers between devices with their start and end apart: 6, of which 4 were waited for; matrix products, arithmetic and copies ran while one was open for 0% of the time, Pallas kernels for 0%

profile of v1, /device:TPU:1, one launch (start us, length us, event | category | flops | bytes accessed | tf_op | source)
XLA Modules:
  0.0 591.6 jit_solution(2314426309738036667)
XLA Ops:
  8.3 0.9 fusion.1
  9.8 4.6 collective-permute-start
  14.4 5.5 collective-permute-start.1
  21.1 3.1 collective-permute-start.2
  24.1 11.7 %collective-permute-start.3 = (f32[3,8,2,128]{3,2,1,0:T(2,128)S(1)}, f32[3,8,2,128]{3,2,1,0:T(2,128)S(1)}, u32[]{:S(2)}, u32[]{:S(2)}) collective-permute-start(f32[3,8,2,128]{3,2,1,0:T(2,128)S(1)} %convolution_bitcast_fusion.1), channel_id=1, source_target_pairs={{8,0},{16,8},{24,16},{32,24},{40,32},{48,40},{56,48},{64,56},{72,6... | collective-permute-start | bytes 73736 | tf_op jit(solution)/shard_map/ppermute | solution.py:19
  35.9 0.8 collective-permute-done.3
  37.3 1.9 fusion.25
  39.8 262.1 %all-reduce.6.cloned.1.call-done = f32[513,513]{0,1:T(8,128)} async-done(((f32[513,513]{0,1:T(8,128)}), f32[513,513]{0,1:T(8,128)}) %all-reduce.6.cloned.1.call-update) | async-done | bytes 1052692 | tf_op jit(solution)/shard_map/psum | solution.py:51
  301.9 1.4 fusion.24
  303.3 82.2 %all-reduce.8.cloned.1.call-done = f32[513,513]{0,1:T(8,128)} async-done(((f32[513,513]{0,1:T(8,128)}), f32[513,513]{0,1:T(8,128)}) %all-reduce.8.cloned.1.call-update) | async-done | bytes 1052692 | tf_op jit(solution)/shard_map/psum | solution.py:50
  385.5 2.5 broadcast_multiply_fusion
  388.0 1.9 copy.56
  390.2 1.0 copy-done.4
  391.7 11.7 %cholesky.131 = f32[128,128]{1,0:T(8,128)S(1)} custom-call(f32[128,128]{1,0:T(8,128)S(1)} %cholesky.333), custom_call_target="Cholesky" | custom-call | tf_op jit(solution)/shard_map/jit(cholesky)/cholesky | solution.py:55
  403.5 9.8 %custom-call.35 = f32[1,128,128]{1,2,0:T(8,128)S(1)} custom-call(f32[1,128,128]{2,1,0:T(8,128)S(1)} %get-tuple-element.47), custom_call_target="InvertDiagBlocksLowerTriangular" | custom-call | tf_op jit(solution)/shard_map/jit(cholesky)/cholesky | solution.py:55
  413.4 1.4 constant_dynamic-update-slice_fusion.2
  414.8 1.4 convolution_subtract_fusion.3
  416.2 11.7 %cholesky.264 = f32[128,128]{1,0:T(8,128)S(1)} custom-call(f32[128,128]{1,0:T(8,128)S(1)} %cholesky.337), custom_call_target="Cholesky" | custom-call | tf_op jit(solution)/shard_map/jit(cholesky)/cholesky | solution.py:55
  428.0 9.9 %custom-call.36 = f32[1,128,128]{1,2,0:T(8,128)S(1)} custom-call(f32[1,128,128]{2,1,0:T(8,128)S(1)} %get-tuple-element.44), custom_call_target="InvertDiagBlocksLowerTriangular" | custom-call | tf_op jit(solution)/shard_map/jit(cholesky)/cholesky | solution.py:55
  438.3 1.3 convolution_subtract_fusion.4
  439.6 11.7 %cholesky.285 = f32[128,128]{1,0:T(8,128)S(1)} custom-call(f32[128,128]{1,0:T(8,128)S(1)} %cholesky.342), custom_call_target="Cholesky" | custom-call | tf_op jit(solution)/shard_map/jit(cholesky)/cholesky | solution.py:55
  451.4 9.8 %custom-call.37 = f32[1,128,128]{1,2,0:T(8,128)S(1)} custom-call(f32[1,128,128]{2,1,0:T(8,128)S(1)} %get-tuple-element.41), custom_call_target="InvertDiagBlocksLowerTriangular" | custom-call | tf_op jit(solution)/shard_map/jit(cholesky)/cholesky | solution.py:55
  461.4 1.3 convolution_subtract_fusion.5
  462.7 11.9 %cholesky.304 = f32[128,128]{1,0:T(8,128)S(1)} custom-call(f32[128,128]{1,0:T(8,128)S(1)} %cholesky.347), custom_call_target="Cholesky" | custom-call | tf_op jit(solution)/shard_map/jit(cholesky)/cholesky | solution.py:55
  474.7 9.8 %custom-call.38 = f32[1,128,128]{1,2,0:T(8,128)S(1)} custom-call(f32[1,128,128]{2,1,0:T(8,128)S(1)} %get-tuple-element.38), custom_call_target="InvertDiagBlocksLowerTriangular" | custom-call | tf_op jit(solution)/shard_map/jit(cholesky)/cholesky | solution.py:55
  491.4 1.3 fusion.20
  493.2 10.6 %while.1 = (s32[]{:T(128)}, f32[513,513]{1,0:T(8,128)S(1)}, s32[4,2]{0,1:T(2,128)S(1)}, f32[4,128,128]{2,1,0:T(8,128)}, s32[]{:T(128)}) while((s32[]{:T(128)}, f32[513,513]{1,0:T(8,128)S(1)}, s32[4,2]{0,1:T(2,128)S(1)}, f32[4,128,128]{2,1,0:T(8,128)}, s32[]{:T(128)}) %tuple.44), condition=%wide.while_cond, body=%wide.while_body.sunk | while | flops 2 | bytes 132705 | solution.py:56
  493.8 2.0 bitcast_dynamic-update-slice_fusion.2
  496.5 2.0 bitcast_dynamic-update-slice_fusion.2
  499.1 2.0 bitcast_dynamic-update-slice_fusion.2
  501.7 2.0 bitcast_dynamic-update-slice_fusion.2
  504.5 1.0 pad_maximum_fusion.3
  505.4 49.1 %custom-call.39 = f32[5,128,128]{1,2,0:T(8,128)S(1)} custom-call(f32[5,128,128]{2,1,0:T(8,128)S(1)} %pad_maximum_fusion.3), custom_call_target="InvertDiagBlocksLowerTriangular" | custom-call | tf_op jit(solution)/shard_map/triangular_solve | solution.py:56
  554.6 2.1 bitcast_convert_fusion
  557.2 2.0 convolution_subtract_fusion.1
  559.2 2.1 fusion.73
  561.3 1.2 copy.57
  562.5 2.3 convolution_subtract_fusion.2
  564.8 2.1 fusion.72
  566.9 1.9 copy.59
  568.8 3.1 convolution_subtract_fusion
  571.9 2.1 fusion.71
  574.0 1.9 copy.66
  575.9 2.0 fusion.17
  578.0 0.9 fusion.28
  579.5 1.1 copy.77
  580.6 2.9 copy.69
  583.5 1.0 pad_maximum_fusion.1
  (79 shorter events, 13.5 us)
Async XLA Ops:
  7.2 2.1 copy-start
  7.2 294.6 %all-reduce.6.cloned.1.call-start = ((), (), s32[]{:S(2)}) async-start(), calls=%async_computation | async-start | bytes 2662400 | tf_op jit(solution)/shard_map/psum | solution.py:51
  9.2 28.1 %copy-start.5 = (bf16[3,1,2,128,512]{4,3,2,1,0:T(8,128)(2,1)S(1)}, bf16[3,1,2,128,512]{4,3,2,1,0:T(8,128)(2,1)}, u32[]{:S(2)}) copy-start(bf16[3,1,2,128,512]{4,3,2,1,0:T(8,128)(2,1)} %param.4) | copy-start | bytes 2359300
  9.8 10.3 %collective-permute-start = (f32[3,8,8,128]{3,2,1,0:T(8,128)S(1)}, f32[3,8,8,128]{3,2,1,0:T(8,128)S(1)}, u32[]{:S(2)}, u32[]{:S(2)}) collective-permute-start(f32[3,8,8,128]{3,2,1,0:T(8,128)S(1)} %get-tuple-element.35), channel_id=1, source_target_pairs={{0,1},{1,2},{2,3},{3,4},{4,5},{5,6},{6,7},{8,9},{9,10},{10,11},{11... | collective-permute-start | bytes 294920 | tf_op jit(solution)/shard_map/ppermute | solution.py:16
  14.4 6.4 %collective-permute-start.1 = (f32[3,8,8,128]{3,2,1,0:T(8,128)S(1)}, f32[3,8,8,128]{3,2,1,0:T(8,128)S(1)}, u32[]{:S(2)}, u32[]{:S(2)}) collective-permute-start(f32[3,8,8,128]{3,2,1,0:T(8,128)S(1)} %get-tuple-element.36), channel_id=1, source_target_pairs={{1,0},{2,1},{3,2},{4,3},{5,4},{6,5},{7,6},{9,8},{10,9},{11,10},{12... | collective-permute-start | bytes 294920 | tf_op jit(solution)/shard_map/ppermute | solution.py:19
  21.1 14.9 %collective-permute-start.2 = (f32[3,8,2,128]{3,2,1,0:T(2,128)S(1)}, f32[3,8,2,128]{3,2,1,0:T(2,128)S(1)}, u32[]{:S(2)}, u32[]{:S(2)}) collective-permute-start(f32[3,8,2,128]{3,2,1,0:T(2,128)S(1)} %convolution_bitcast_fusion.1), channel_id=1, source_target_pairs={{0,8},{8,16},{16,24},{24,32},{32,40},{40,48},{48,56},{56,64},{64,7... | collective-permute-start | bytes 73736 | tf_op jit(solution)/shard_map/ppermute | solution.py:16
  24.1 12.6 %collective-permute-start.3 = (f32[3,8,2,128]{3,2,1,0:T(2,128)S(1)}, f32[3,8,2,128]{3,2,1,0:T(2,128)S(1)}, u32[]{:S(2)}, u32[]{:S(2)}) collective-permute-start(f32[3,8,2,128]{3,2,1,0:T(2,128)S(1)} %convolution_bitcast_fusion.1), channel_id=1, source_target_pairs={{8,0},{16,8},{24,16},{32,24},{40,32},{48,40},{56,48},{64,56},{72,6... | collective-permute-start | bytes 73736 | tf_op jit(solution)/shard_map/ppermute | solution.py:19
  39.2 346.3 %all-reduce.8.cloned.1.call-start = ((), (), s32[]{:S(2)}) async-start(), calls=%async_computation.1 | async-start | bytes 2662400 | tf_op jit(solution)/shard_map/psum | solution.py:50
  388.0 1.9 copy-start.2
  390.1 1.1 copy-start.4
  503.7 53.5 %copy-start.3 = (f32[513,513]{1,0:T(8,128)}, f32[513,513]{1,0:T(8,128)S(1)}, u32[]{:S(2)}) copy-start(f32[513,513]{1,0:T(8,128)S(1)} %get-tuple-element.110) | copy-start | bytes 3158032
  554.6 2.6 copy-start.9
  557.2 5.2 copy-start.1
  580.6 3.0 copy-start.6
  580.6 2.9 copy-start.7
  580.6 2.9 copy-start.8
Sparse Core Ops, SparseCore 0:
  39.4 262.4 all-reduce.5
  304.2 81.2 all-reduce.7
